TPU v7x, 32 devices: a whole 2x2x4 slice. The times are simulated.
32 devices in a mesh: tile: 8 (over y, x, core), depth: 4 (over z).
Axes of the slice: x: 2, y: 2, z: 4, core: 2. Of those that a mesh axis runs over, the one named last changes fastest.
Arguments:
- coefficients: float32 [8, 4, 8, 32, 128], P(None, 'depth', 'tile'), may hold values from -24 to 24
- keep_count: int32 [4, 8, 32, 128], P('depth', 'tile'), may hold values from 1 to 8, as said below
- view_flip: int32 [8], P('tile'), may hold values from 0 to 1
Outputs:
- image: float32 [4, 128, 512], P(None, 'tile', 'depth')
Inputs may be any that keep to these rules, and one draw needn't show every extreme that they name: `keep_count`: along the block rows, blocks 2 j and 2 j + 1 of every brick and block column retain 8 + 1 slots together.
All inputs are finite; a program needn't handle non-finite values.
Results may differ from a plain program's by a relative error of at most 0.0003.
Values sent between devices are 32-bit elements; how exact they have to be, the bound alone decides.
No kernel may reach another device: no remote copies, remote signals or barrier semaphores. Data moves between devices by JAX's collectives and lax.ppermute only.
A program may use at most 64 MiB of HBM per device.

v0:
```python
import math

import jax
import jax.numpy as jnp
import numpy as np
from jax import lax
from jax.sharding import PartitionSpec as P

slot_frequencies = (
    (0, 0, 0),
    (0, 0, 1),
    (0, 1, 0),
    (1, 0, 0),
    (0, 0, 2),
    (0, 1, 1),
    (0, 2, 0),
    (1, 0, 1),
)


def cosine_rows():
    result = np.zeros((4, 4))
    for frequency in range(4):
        factor = 0.5 if frequency == 0 else math.sqrt(0.5)
        for position in range(4):
            result[frequency, position] = factor * math.cos(
                math.pi * (2 * position + 1) * frequency / 8.0
            )
    return result


def basis_matrix(slot_count):
    rows_table = cosine_rows()
    result = np.zeros((4, 4, 4, slot_count))
    for slot_index in range(slot_count):
        freq_z, freq_x, freq_y = slot_frequencies[slot_index]
        result[:, :, :, slot_index] = (
            rows_table[freq_z][:, None, None]
            * rows_table[freq_x][None, :, None]
            * rows_table[freq_y][None, None, :]
        )
    return jnp.asarray(result.reshape(64, slot_count), dtype=jnp.float32)


def render_columns(block_coef, basis_rows, flipped, sample_count):
    slot_count, zblocks, column_count = block_coef.shape
    flat_coef = block_coef.reshape(slot_count, zblocks * column_count)
    cell_values = jnp.dot(
        basis_rows, flat_coef, precision=lax.Precision.HIGHEST, preferred_element_type=jnp.float32
    )
    cell_values = cell_values.reshape(4, 16, zblocks, column_count)
    density = jnp.transpose(cell_values, (2, 0, 1, 3)).reshape(zblocks * 4, 16, column_count)
    optical = 1.5 * jax.nn.softplus(2.0 * density) / sample_count
    inclusive = jnp.cumsum(optical, axis=0)
    total_depth = inclusive[-1]
    entering = jnp.where(flipped > 0, total_depth[None] - inclusive, inclusive - optical)
    weights = jnp.exp(-entering) * -jnp.expm1(-optical)
    red_sum = jnp.sum(weights * jax.nn.sigmoid(2.0 * density), axis=0)
    green_sum = jnp.sum(weights * jnp.exp(-density * density), axis=0)
    blue_sum = jnp.sum(weights * jax.nn.sigmoid(1.5 - density), axis=0)
    opacity = -jnp.expm1(-total_depth)
    return jnp.stack([red_sum, green_sum, blue_sum, opacity])


def to_image(layer, strip_blocks, column_blocks):
    spread = layer.reshape(4, 4, 4, strip_blocks, column_blocks)
    return jnp.transpose(spread, (0, 3, 1, 4, 2)).reshape(4, strip_blocks * 4, column_blocks * 4)


def composite(layers, flipped, layer_axis):
    clearance = 1.0 - layers[3:4]
    piece_count = layers.shape[layer_axis]
    forward = jnp.cumprod(clearance, axis=layer_axis)
    backward = jnp.flip(jnp.cumprod(jnp.flip(clearance, layer_axis), axis=layer_axis), layer_axis)
    unit_slice = jnp.ones_like(lax.slice_in_dim(clearance, 0, 1, axis=layer_axis))
    before_forward = jnp.concatenate(
        [unit_slice, lax.slice_in_dim(forward, 0, piece_count - 1, axis=layer_axis)],
        axis=layer_axis,
    )
    before_backward = jnp.concatenate(
        [lax.slice_in_dim(backward, 1, piece_count, axis=layer_axis), unit_slice], axis=layer_axis
    )
    passing = jnp.where(flipped > 0, before_backward, before_forward)
    return jnp.sum(passing * layers, axis=layer_axis)


def per_device(coefficients, keep_count, view_flip):
    slot_count = coefficients.shape[0]
    tile_count = lax.axis_size("tile")
    depth_count = lax.axis_size("depth")
    column_blocks = coefficients.shape[4]
    local_columns = coefficients.shape[3]
    strip_blocks = local_columns // tile_count
    flipped = view_flip[0]
    basis_rows = basis_matrix(slot_count)
    sample_count = 4 * tile_count * depth_count
    slot_index = lax.broadcasted_iota(jnp.int32, coefficients.shape, 0)
    masked = jnp.where(slot_index < keep_count[None], coefficients, jnp.float32(0.0))
    outgoing = masked.reshape(slot_count, 1, tile_count, strip_blocks * column_blocks)
    layer = render_columns(
        lax.all_to_all(outgoing, "tile", split_axis=2, concat_axis=1, tiled=True)[:, :, 0, :],
        basis_rows,
        flipped,
        sample_count,
    )
    picture = to_image(layer, strip_blocks, column_blocks)
    strip_width = picture.shape[1]
    band_rows = picture.shape[2] // depth_count
    pieces = picture.reshape(4, strip_width, depth_count, band_rows)
    gathered = lax.all_to_all(pieces, "depth", split_axis=2, concat_axis=2, tiled=True)
    return composite(gathered, flipped, 2)


def solution(mesh):
    placed = (P(None, "depth", "tile", None, None), P("depth", "tile", None, None), P("tile"))
    return jax.shard_map(
        per_device, mesh=mesh, in_specs=placed, out_specs=P(None, "tile", "depth"), check_vma=False
    )
```

profile of v0, /device:TPU:0, one launch (start us, length us, event | category | flops | bytes accessed | tf_op | source)
XLA Modules:
  0.0 37.9 jit_solution(1767945038892745813)
XLA Ops:
  0.0 0.9 %fusion.20 = f32[8,1,1,32,128]{4,3,2,1,0:T(8,128)S(1)} fusion(f32[8,1,1,32,128]{4,3,2,1,0:T(8,128)} %param.4, s32[32,128]{1,0:T(8,128)} %bitcast.99), kind=kLoop, calls=%fused_computation.30 | loop fusion | flops 65536 | bytes 278528 | tf_op jit(solution)/shard_map/jit(_where)/select_n | solution.py:98
  1.0 0.7 %copy.21 = f32[8,1,8,512]{3,0,1,2:T(8,128)} copy(f32[8,1,8,512]{3,2,0,1:T(8,128)S(1)} %reshape.37) | data formatting | bytes 262144 | tf_op jit(solution)/shard_map/reshape | solution.py:99
  1.7 5.2 %all-to-all-start = ((f32[8,1,8,512]{3,0,1,2:T(8,128)}), f32[8,1,8,512]{3,0,1,2:T(8,128)S(1)}, u32[]{:S(2)}, u32[]{:S(2)}) async-start(f32[8,1,8,512]{3,0,1,2:T(8,128)} %copy.21), calls=%async_computation | async-start | bytes 262144 | tf_op jit(solution)/shard_map/all_to_all | solution.py:101
  7.5 4.9 %all-to-all-done = f32[8,1,8,512]{3,0,1,2:T(8,128)S(1)} async-done(((f32[8,1,8,512]{3,0,1,2:T(8,128)}), f32[8,1,8,512]{3,0,1,2:T(8,128)S(1)}, u32[]{:S(2)}, u32[]{:S(2)}) %all-to-all-start) | async-done | bytes 131104 | tf_op jit(solution)/shard_map/all_to_all | solution.py:101
  12.4 1.7 %fusion.31 = f32[64,4096]{1,0:T(8,128)S(1)} fusion(f32[64,8]{1,0:T(8,128)} %constant.28.clone, f32[8,4096]{1,0:T(8,128)S(1)} %bitcast.98), kind=kOutput, calls=%fused_computation.44 | convolution fusion | flops 25165824 | bytes 1181696 | tf_op jit(solution)/shard_map/dot_general | solution.py:48
  14.1 0.6 %copy.27 = f32[8,8,8,512]{3,2,1,0:T(8,128)S(1)} copy(f32[8,8,8,512]{3,1,2,0:T(8,128)S(1)} %bitcast.96) | data formatting | bytes 2097152
  14.7 0.1 fusion.8
  14.8 0.6 %copy.22 = f32[8,4,16,512]{3,2,1,0:T(8,128)S(1)} copy(f32[8,4,16,512]{3,0,2,1:T(8,128)S(1)} %fusion.8) | data formatting | bytes 2097152 | tf_op jit(solution)/shard_map/mul | solution.py:53
  15.4 0.5 %fusion.14 = f32[32,16,512]{2,1,0:T(8,128)S(1)} fusion(f32[8,4,16,512]{3,2,1,0:T(8,128)S(1)} %copy.22), kind=kLoop, calls=%fused_computation.19 | loop fusion | flops 1048576 | bytes 2097152 | tf_op jit(solution)/shard_map/jit(softplus)/add | solution.py:53
  15.9 0.4 %fusion.4 = f32[32,16,512]{2,1,0:T(8,128)S(1)} fusion(f32[32,16,512]{2,1,0:T(8,128)S(1)} %bitcast.93, f32[32,16,512]{2,1,0:T(8,128)S(1)} %fusion.14), kind=kOutput, calls=%fused_computation.7 | output fusion | flops 8912896 | bytes 3145728 | tf_op jit(solution)/shard_map/jit(cumsum)/reduce_window_sum | solution.py:54
  16.4 2.3 %multiply_reduce_fusion = (f32[16,512]{1,0:T(8,128)S(1)}, f32[16,512]{1,0:T(8,128)S(1)}, f32[16,512]{1,0:T(8,128)S(1)}) fusion(f32[8,4,16,512]{3,2,1,0:T(8,128)S(1)} %bitcast.97, f32[16,512]{1,0:T(8,128)S(1)} %get-tuple-element.8, pred[]{:T(512)} %bitcast, f32[4,16,8,512]{3,2,1,0:T(8,128)S(1)} %bitcast.95), kind=kLoop, calls=%fused_computation.23 | loop fusion | flops 7839744 | bytes 2228225 | tf_op jit(solution)/shard_map/reduce_sum | solution.py:58
  18.8 2.6 %copy.25 = f32[4,4,4,128,4]{4,3,2,1,0:T(8,128)} copy(f32[4,4,4,128,4]{3,1,4,2,0:T(4,128)S(1)} %maximum_bitcast_fusion) | data formatting | bytes 262144 | tf_op jit(solution)/shard_map/transpose | solution.py:67
  21.4 4.9 %reshape_reshape.3 = f32[4,16,4,128]{3,2,1,0:T(4,128)S(1)} reshape(f32[4,4,4,128,4]{4,3,2,1,0:T(8,128)} %copy.25) | data formatting | bytes 262144 | tf_op jit(solution)/shard_map/reshape;reshape | solution.py:109
  26.4 10.7 %all_to_all.14 = f32[4,16,4,128]{3,1,0,2:T(8,128)S(1)} all-to-all(f32[4,16,4,128]{3,1,0,2:T(8,128)S(1)} %copy.26), channel_id=1, replica_groups=mesh['tile'=8,'depth'=4] {'depth'}, dimensions={2} | all-to-all | bytes 262144 | tf_op jit(solution)/shard_map/all_to_all | solution.py:110
  37.2 0.6 %multiply_reduce_fusion.1 = f32[4,16,128]{2,1,0:T(8,128)} fusion(f32[4,16,4,128]{3,1,0,2:T(8,128)S(1)} %all_to_all.14, f32[16,4,128]{2,0,1:T(8,128)S(1)} %select_bitcast_fusion), kind=kLoop, calls=%fused_computation.28 | loop fusion | flops 57344 | bytes 196608 | tf_op jit(solution)/shard_map/reduce_sum | solution.py:84
  (16 shorter events, 0.2 us)
Async XLA Ops:
  1.7 10.7 %all-to-all-start = ((f32[8,1,8,512]{3,0,1,2:T(8,128)}), f32[8,1,8,512]{3,0,1,2:T(8,128)S(1)}, u32[]{:S(2)}, u32[]{:S(2)}) async-start(f32[8,1,8,512]{3,0,1,2:T(8,128)} %copy.21), calls=%async_computation | async-start | bytes 262144 | tf_op jit(solution)/shard_map/all_to_all | solution.py:101
where the time goes:
time: 38.2 us; the launch traced here: 37.9 us
  blocking collectives  10.7 us (28%)
  local copies, waits for them, and re-layouts  9.6 us (25%)
  starting transfers between devices  5.17 us (14%)
  other arithmetic  4.95 us (13%)
  waiting for transfers between devices  4.88 us (13%)
  matrix products  1.7 us (4%)
  between operations  0.82 us (2%)
    all_to_all x1, blocking collectives, per_device(): lax.all_to_all(pieces, 'depth', split_axis=2, concat_axis=2, tiled=True)  10.7 us
    all_to_all x1, starting transfers between devices, per_device(): lax.all_to_all(outgoing, 'tile', split_axis=2, concat_axis=1, tiled=True)  5.17 us
    another operation x2, local copies, waits for them, and re-layouts, per_device(): pieces = picture.reshape(4, strip_width, depth_count, band_rows)  4.94 us
    all_to_all x1, waiting for transfers between devices, per_device(): lax.all_to_all(outgoing, 'tile', split_axis=2, concat_axis=1, tiled=True)  4.88 us
    transpose x1, local copies, waits for them, and re-layouts, to_image(): jnp.transpose(spread, (0, 3, 1, 4, 2))  2.62 us
    reduce_sum x1, other arithmetic, render_columns(): red_sum = jnp.sum(weights * jax.nn.sigmoid(2.0 * density), axis=0)  2.33 us
    dot_general x1, matrix products, render_columns(): jnp.dot(basis_rows, flat_coef, precision=lax.Precision.HIGHEST, preferred...  1.7 us
    select_n x1, other arithmetic, per_device(): jnp.where(slot_index < keep_count[None], coefficients, jnp.float32(0.0))  0.92 us
  transfers between devices with their start and end apart: 1, of which 1 were waited for; matrix products, arithmetic and copies ran while one was open for 0% of the time, Pallas kernels for 0%

commit v1 on v0

v1 whole, which is shorter than its diff:
```python
import math

import jax
import jax.numpy as jnp
from jax import lax
from jax.experimental import pallas as pl
from jax.experimental.pallas import tpu as pltpu
from jax.sharding import PartitionSpec as P

LOG2E = math.log2(math.e)
EDGE = 4


def cosine(frequency, position):
    factor = 0.5 if frequency == 0 else math.sqrt(0.5)
    return factor * math.cos(math.pi * (2 * position + 1) * frequency / 8.0)


def pack_kernel(coef_ref, keep_ref, out_ref, *, tiles, depths):
    slots, columns, rows = coef_ref.shape
    strip = columns // tiles
    band = rows // depths
    slot_index = lax.broadcasted_iota(jnp.int32, (slots, rows), 0)
    for t in range(tiles):
        masked = []
        for b in range(strip):
            c = t * strip + b
            keep = jnp.broadcast_to(keep_ref[pl.ds(c, 1), :], (slots, rows))
            masked.append(jnp.where(slot_index < keep, coef_ref[:, c, :], 0.0))
        for d in range(depths):
            out_ref[d * tiles + t] = jnp.concatenate(
                [m[:, d * band : (d + 1) * band] for m in masked], axis=1
            )


def render_kernel(flip_ref, coef_ref, out_ref, *, strip, band, samples):
    zblocks, slots, lanes = coef_ref.shape
    flipped = flip_ref[0] > 0
    b1 = [cosine(1, i) for i in range(EDGE)]
    row = lax.broadcasted_iota(jnp.int32, (2 * EDGE, lanes), 0)
    x = row % EDGE
    y = row // EDGE

    def table(position, values):
        result = jnp.full((2 * EDGE, lanes), values[0], jnp.float32)
        for i in range(1, len(values)):
            result = jnp.where(position == i, jnp.float32(values[i]), result)
        return result

    x1 = table(x, b1)
    x2 = table(x, [cosine(2, i) for i in range(EDGE)])
    y1 = table(y, b1[:2])
    y2 = table(y, [cosine(2, i) for i in range(2)])
    sign = jnp.where(flipped, jnp.float32(-1.0), jnp.float32(1.0))
    c_dc = 0.125 * LOG2E
    c_x1 = (0.25 * LOG2E) * x1
    c_x2 = (0.25 * LOG2E) * x2
    c_y1 = (0.25 * LOG2E) * y1
    c_y2 = (0.25 * LOG2E) * y2
    c_xy = (0.5 * LOG2E) * x1 * y1
    c_z = jnp.full((2 * EDGE, lanes), 0.25 * LOG2E * b1[0], jnp.float32) * sign
    c_zy = (0.5 * LOG2E * b1[0]) * y1 * sign
    ratio = b1[1] / b1[0]
    blue_factor = math.exp(-1.5)
    fade = -1.5 / samples

    def block(step, state):
        zb = jnp.where(flipped, zblocks - 1 - step, step)
        a = [
            jnp.broadcast_to(coef_ref[zb, pl.ds(k, 1), :], (2 * EDGE, lanes)) for k in range(slots)
        ]
        even = a[0] * c_dc + a[2] * c_x1 + a[4] * c_y2 + a[6] * c_x2
        odd = a[1] * c_y1 + a[5] * c_xy
        g_even = a[3] * c_z
        g_odd = a[7] * c_zy
        halves = []
        for h in range(2):
            depth, before, red, green, blue = state[h]
            base = even + odd if h == 0 else even - odd
            g = g_even + g_odd if h == 0 else g_even - g_odd
            near = g * ratio
            for f in (base + g, base + near, base - near, base - g):
                v = jnp.exp2(f)
                one_u = 1.0 + v * v
                depth = depth + jnp.log2(one_u)
                after = jnp.exp2(fade * depth)
                weight = before - after
                before = after
                red = red + weight / one_u
                green = green + weight * jnp.exp2(f * (f * (-1.0 / LOG2E)))
                blue = blue + weight / (1.0 + blue_factor * v)
            halves.append((depth, before, red, green, blue))
        return tuple(halves)

    zero = jnp.zeros((2 * EDGE, lanes), jnp.float32)
    one = jnp.ones((2 * EDGE, lanes), jnp.float32)
    start = (zero, one, zero, zero, zero)
    state = lax.fori_loop(0, zblocks, block, (start, start), unroll=4)

    width = band * EDGE
    pick = lax.broadcasted_iota(jnp.int32, (2 * EDGE, width), 1)
    y_out = pick % EDGE
    place = pick // EDGE
    outs = []
    for _, before, red, green, blue in state:
        opacity = 1.0 - before
        outs.append((opacity - red, green, blue, opacity))
    for ch in range(4):
        for b in range(strip):
            index = place + b * band
            low = jnp.take_along_axis(outs[0][ch], index, axis=1)
            high = jnp.take_along_axis(outs[1][ch], index, axis=1)
            both = jnp.where(y_out < 2, low, high)
            first, second = both[:EDGE], both[EDGE:]
            use_first = (y_out[:EDGE] == 0) | (y_out[:EDGE] == 3)
            out_ref[ch, pl.ds(b * EDGE, EDGE), :] = jnp.where(use_first, first, second)


def per_device(coefficients, keep_count, view_flip):
    tiles = lax.axis_size("tile")
    depths = lax.axis_size("depth")
    slots, _, _, columns, rows = coefficients.shape
    strip = columns // tiles
    band = rows // depths
    zblocks = tiles * depths
    vmem = pl.BlockSpec(memory_space=pltpu.VMEM)
    smem = pl.BlockSpec(memory_space=pltpu.SMEM)
    outgoing = pl.pallas_call(
        lambda *refs: pack_kernel(*refs, tiles=tiles, depths=depths),
        out_shape=jax.ShapeDtypeStruct((zblocks, slots, strip * band), jnp.float32),
        in_specs=[vmem, vmem],
        out_specs=vmem,
        name="pack",
    )(coefficients.reshape(slots, columns, rows), keep_count.reshape(columns, rows))
    arrived = lax.all_to_all(outgoing, ("depth", "tile"), split_axis=0, concat_axis=0, tiled=True)
    return pl.pallas_call(
        lambda *refs: render_kernel(*refs, strip=strip, band=band, samples=EDGE * zblocks),
        out_shape=jax.ShapeDtypeStruct((4, strip * EDGE, band * EDGE), jnp.float32),
        in_specs=[smem, vmem],
        out_specs=vmem,
        name="render",
    )(view_flip, arrived)


def solution(mesh):
    placed = (P(None, "depth", "tile", None, None), P("depth", "tile", None, None), P("tile"))
    return jax.shard_map(
        per_device, mesh=mesh, in_specs=placed, out_specs=P(None, "tile", "depth"), check_vma=False
    )
```

time: 38.2 us -> 20.9 us (0.55)
  blocking collectives: 10.7 us -> 0 us
  local copies, waits for them, and re-layouts: 9.6 us -> 0.65 us
  other arithmetic: 4.95 us -> 0 us
  Pallas kernels: 0 us -> 4.53 us
  waiting for transfers between devices: 4.88 us -> 7.58 us
  starting transfers between devices: 5.17 us -> 7.3 us
  matrix products: 1.7 us -> 0 us
    all_to_all x1 -> x0, blocking collectives: 10.7 us -> none  [per_device(): lax.all_to_all(pieces, 'depth', split_axis=2, concat_axis=2, tiled=True)]
    another operation x7 -> x0, local copies, waits for them, and re-layouts: 5.01 us -> none  [the longest x2 4.94 us: per_device(): pieces = picture.reshape(4, strip_width, depth_count, band_rows)]
    pallas_call x0 -> x2, Pallas kernels: none -> 4.53 us  [the longest x1 2.8 us: per_device(): pl.pallas_call(lambda *refs: render_kernel(*refs, strip=strip, band=band,...]
    reduce_sum x2 -> x0, other arithmetic: 2.96 us -> none  [the longest x1 2.33 us: render_columns(): red_sum = jnp.sum(weights * jax.nn.sigmoid(2.0 * density), axis=0)]
    all_to_all x1, waiting for transfers between devices: 4.88 us -> 7.58 us  [per_device(): lax.all_to_all(outgoing, ('depth', 'tile'), split_axis=0, concat_axis=0,...]
    transpose x1 -> x0, local copies, waits for them, and re-layouts: 2.62 us -> none  [to_image(): jnp.transpose(spread, (0, 3, 1, 4, 2))]
    all_to_all x1, starting transfers between devices: 5.17 us -> 7.3 us  [per_device(): lax.all_to_all(outgoing, ('depth', 'tile'), split_axis=0, concat_axis=0,...]
    dot_general x1 -> x0, matrix products: 1.7 us -> none  [render_columns(): jnp.dot(basis_rows, flat_coef, precision=lax.Precision.HIGHEST, preferred...]
where the time goes in v1:
time: 20.9 us; the launch traced here: 20.7 us
  waiting for transfers between devices  7.58 us (36%)
  starting transfers between devices  7.3 us (35%)
  Pallas kernels  4.53 us (22%)
  between operations  0.66 us (3%)
  local copies, waits for them, and re-layouts  0.65 us (3%)
    all_to_all x1, waiting for transfers between devices, per_device(): lax.all_to_all(outgoing, ('depth', 'tile'), split_axis=0, concat_axis=0,...  7.58 us
    all_to_all x1, starting transfers between devices, per_device(): lax.all_to_all(outgoing, ('depth', 'tile'), split_axis=0, concat_axis=0,...  7.3 us
    pallas_call x1, Pallas kernels, per_device(): pl.pallas_call(lambda *refs: render_kernel(*refs, strip=strip, band=band,...  2.8 us
    pallas_call x1, Pallas kernels, per_device(): pl.pallas_call(lambda *refs: pack_kernel(*refs, tiles=tiles, depths=depth...  1.73 us
    unnamed x2, local copies, waits for them, and re-layouts  0.65 us
  transfers between devices with their start and end apart: 1, of which 1 were waited for; matrix products, arithmetic and copies ran while one was open for 0% of the time, Pallas kernels for 0%

profile of v1, /device:TPU:0, one launch (start us, length us, event | category | flops | bytes accessed | tf_op | source)
XLA Modules:
  0.0 20.7 jit_solution(10395580522628099497)
XLA Ops:
  0.0 1.7 %pack.1 = f32[32,8,128]{2,1,0:T(8,128)} custom-call(f32[8,32,128]{2,1,0:T(8,128)} %bitcast.2, s32[32,128]{1,0:T(8,128)} %bitcast.3), custom_call_target="tpu_custom_call" | custom-call | tf_op jit(solution)/shard_map/pack/pallas_call | solution.py:128
  1.7 7.3 %all-to-all-start = ((f32[32,8,128]{2,1,0:T(8,128)}), f32[32,8,128]{2,1,0:T(8,128)S(1)}, u32[]{:S(2)}, u32[]{:S(2)}) async-start(f32[32,8,128]{2,1,0:T(8,128)} %pack.1), calls=%async_computation | async-start | bytes 262144 | tf_op jit(solution)/shard_map/all_to_all | solution.py:135
  9.7 7.6 %all-to-all-done.refs_1_ = f32[32,8,128]{2,1,0:T(8,128)S(1)} async-done(((f32[32,8,128]{2,1,0:T(8,128)}), f32[32,8,128]{2,1,0:T(8,128)S(1)}, u32[]{:S(2)}, u32[]{:S(2)}) %all-to-all-start) | async-done | bytes 131104 | tf_op jit(solution)/shard_map/all_to_all | solution.py:135
  17.3 0.0 copy-start
  17.3 0.6 %copy-done = f32[32,8,128]{2,1,0:T(8,128)} copy-done((f32[32,8,128]{2,1,0:T(8,128)}, f32[32,8,128]{2,1,0:T(8,128)S(1)}, u32[]{:S(2)}) %copy-start) | copy-done | bytes 131096
  17.9 2.8 %render.1 = f32[4,16,128]{2,1,0:T(8,128)} custom-call(s32[1]{0:T(128)S(6)} %copy.4.refs_0_, f32[32,8,128]{2,1,0:T(8,128)} %copy-done), custom_call_target="tpu_custom_call" | custom-call | tf_op jit(solution)/shard_map/render/pallas_call | solution.py:136
Async XLA Ops:
  1.7 15.5 %all-to-all-start = ((f32[32,8,128]{2,1,0:T(8,128)}), f32[32,8,128]{2,1,0:T(8,128)S(1)}, u32[]{:S(2)}, u32[]{:S(2)}) async-start(f32[32,8,128]{2,1,0:T(8,128)} %pack.1), calls=%async_computation | async-start | bytes 262144 | tf_op jit(solution)/shard_map/all_to_all | solution.py:135
  17.3 0.6 %copy-start = (f32[32,8,128]{2,1,0:T(8,128)}, f32[32,8,128]{2,1,0:T(8,128)S(1)}, u32[]{:S(2)}) copy-start(f32[32,8,128]{2,1,0:T(8,128)S(1)} %all-to-all-done.refs_1_) | copy-start | bytes 393220

commit v2 on v1

--- a/solution.py
+++ b/solution.py
@@ -16,10 +16,18 @@
     return factor * math.cos(math.pi * (2 * position + 1) * frequency / 8.0)
 
 
-def pack_kernel(coef_ref, keep_ref, out_ref, *, tiles, depths):
+def pack_kernel(coef_hbm, keep_hbm, out_ref, coef_ref, keep_ref, arrival, *, tiles, depths):
     slots, columns, rows = coef_ref.shape
     strip = columns // tiles
     band = rows // depths
+    fetches = [
+        pltpu.make_async_copy(coef_hbm, coef_ref, arrival.at[0]),
+        pltpu.make_async_copy(keep_hbm, keep_ref, arrival.at[1]),
+    ]
+    for fetch in fetches:
+        fetch.start()
+    for fetch in fetches:
+        fetch.wait()
     slot_index = lax.broadcasted_iota(jnp.int32, (slots, rows), 0)
     for t in range(tiles):
         masked = []
@@ -36,6 +44,7 @@
 def render_kernel(flip_ref, coef_ref, out_ref, *, strip, band, samples):
     zblocks, slots, lanes = coef_ref.shape
     flipped = flip_ref[0] > 0
+    sign = jnp.where(flipped, jnp.float32(-1.0), jnp.float32(1.0))
     b1 = [cosine(1, i) for i in range(EDGE)]
     row = lax.broadcasted_iota(jnp.int32, (2 * EDGE, lanes), 0)
     x = row % EDGE
@@ -51,7 +60,6 @@
     x2 = table(x, [cosine(2, i) for i in range(EDGE)])
     y1 = table(y, b1[:2])
     y2 = table(y, [cosine(2, i) for i in range(2)])
-    sign = jnp.where(flipped, jnp.float32(-1.0), jnp.float32(1.0))
     c_dc = 0.125 * LOG2E
     c_x1 = (0.25 * LOG2E) * x1
     c_x2 = (0.25 * LOG2E) * x2
@@ -124,20 +132,27 @@
     band = rows // depths
     zblocks = tiles * depths
     vmem = pl.BlockSpec(memory_space=pltpu.VMEM)
-    smem = pl.BlockSpec(memory_space=pltpu.SMEM)
+    params = pltpu.CompilerParams(vmem_limit_bytes=4 * 1024 * 1024)
     outgoing = pl.pallas_call(
         lambda *refs: pack_kernel(*refs, tiles=tiles, depths=depths),
         out_shape=jax.ShapeDtypeStruct((zblocks, slots, strip * band), jnp.float32),
-        in_specs=[vmem, vmem],
+        in_specs=[pl.BlockSpec(memory_space=pltpu.HBM)] * 2,
         out_specs=vmem,
+        scratch_shapes=[
+            pltpu.VMEM((slots, columns, rows), jnp.float32),
+            pltpu.VMEM((columns, rows), jnp.int32),
+            pltpu.SemaphoreType.DMA((2,)),
+        ],
+        compiler_params=params,
         name="pack",
     )(coefficients.reshape(slots, columns, rows), keep_count.reshape(columns, rows))
     arrived = lax.all_to_all(outgoing, ("depth", "tile"), split_axis=0, concat_axis=0, tiled=True)
     return pl.pallas_call(
         lambda *refs: render_kernel(*refs, strip=strip, band=band, samples=EDGE * zblocks),
         out_shape=jax.ShapeDtypeStruct((4, strip * EDGE, band * EDGE), jnp.float32),
-        in_specs=[smem, vmem],
+        in_specs=[pl.BlockSpec(memory_space=pltpu.SMEM), vmem],
         out_specs=vmem,
+        compiler_params=params,
         name="render",
     )(view_flip, arrived)
 

time: 20.9 us -> 20.4 us (0.976)
  Pallas kernels: 4.53 us -> 2.9 us
  local copies, waits for them, and re-layouts: 0.65 us -> 1.62 us
    unnamed x2 -> x4, local copies, waits for them, and re-layouts: 0.65 us -> 1.62 us
    pallas_call x1, Pallas kernels: 2.8 us -> 1.9 us  [per_device(): pl.pallas_call(lambda *refs: render_kernel(*refs, strip=strip, band=band,...]
    pallas_call x1, Pallas kernels: 1.73 us -> 1 us  [per_device(): pl.pallas_call(lambda *refs: pack_kernel(*refs, tiles=tiles, depths=depth...]
where the time goes in v2:
time: 20.4 us; the launch traced here: 20.1 us
  waiting for transfers between devices  7.58 us (37%)
  starting transfers between devices  7.3 us (36%)
  Pallas kernels  2.9 us (14%)
  local copies, waits for them, and re-layouts  1.62 us (8%)
  between operations  0.67 us (3%)
    all_to_all x1, waiting for transfers between devices, per_device(): lax.all_to_all(outgoing, ('depth', 'tile'), split_axis=0, concat_axis=0,...  7.58 us
    all_to_all x1, starting transfers between devices, per_device(): lax.all_to_all(outgoing, ('depth', 'tile'), split_axis=0, concat_axis=0,...  7.3 us
    pallas_call x1, Pallas kernels, per_device(): pl.pallas_call(lambda *refs: render_kernel(*refs, strip=strip, band=band,...  1.9 us
    unnamed x4, local copies, waits for them, and re-layouts  1.62 us
    pallas_call x1, Pallas kernels, per_device(): pl.pallas_call(lambda *refs: pack_kernel(*refs, tiles=tiles, depths=depth...  1 us
  transfers between devices with their start and end apart: 1, of which 1 were waited for; matrix products, arithmetic and copies ran while one was open for 0% of the time, Pallas kernels for 0%

profile of v2, /device:TPU:0, one launch (start us, length us, event | category | flops | bytes accessed | tf_op | source)
XLA Modules:
  0.0 20.1 jit_solution(7769609085729454947)
XLA Ops:
  0.0 0.0 copy-start
  0.0 0.9 %copy-done = f32[8,1,1,32,128]{4,3,2,1,0:T(8,128)S(1)} copy-done((f32[8,1,1,32,128]{4,3,2,1,0:T(8,128)S(1)}, f32[8,1,1,32,128]{4,3,2,1,0:T(8,128)}, u32[]{:S(2)}) %copy-start) | copy-done | bytes 131096
  0.9 0.0 copy-start.1
  0.9 0.7 %copy-done.1 = s32[1,1,32,128]{3,2,1,0:T(8,128)S(1)} copy-done((s32[1,1,32,128]{3,2,1,0:T(8,128)S(1)}, s32[1,1,32,128]{3,2,1,0:T(8,128)}, u32[]{:S(2)}) %copy-start.1) | copy-done | bytes 16408
  1.6 1.0 %pack.1 = f32[32,8,128]{2,1,0:T(8,128)} custom-call(f32[8,32,128]{2,1,0:T(8,128)S(1)} %bitcast.2, s32[32,128]{1,0:T(8,128)S(1)} %bitcast.3), custom_call_target="tpu_custom_call" | custom-call | tf_op jit(solution)/shard_map/pack/pallas_call | solution.py:136
  2.6 7.3 %all-to-all-start = ((f32[32,8,128]{2,1,0:T(8,128)}), f32[32,8,128]{2,1,0:T(8,128)S(1)}, u32[]{:S(2)}, u32[]{:S(2)}) async-start(f32[32,8,128]{2,1,0:T(8,128)} %pack.1), calls=%async_computation | async-start | bytes 262144 | tf_op jit(solution)/shard_map/all_to_all | solution.py:149
  10.6 7.6 %all-to-all-done.refs_1_ = f32[32,8,128]{2,1,0:T(8,128)S(1)} async-done(((f32[32,8,128]{2,1,0:T(8,128)}), f32[32,8,128]{2,1,0:T(8,128)S(1)}, u32[]{:S(2)}, u32[]{:S(2)}) %all-to-all-start) | async-done | bytes 131104 | tf_op jit(solution)/shard_map/all_to_all | solution.py:149
  18.2 1.9 %render.1 = f32[4,16,128]{2,1,0:T(8,128)} custom-call(s32[1]{0:T(128)S(6)} %copy.4.refs_0_, f32[32,8,128]{2,1,0:T(8,128)S(1)} %all-to-all-done.refs_1_), custom_call_target="tpu_custom_call" | custom-call | tf_op jit(solution)/shard_map/render/pallas_call | solution.py:150
Async XLA Ops:
  0.0 0.9 %copy-start = (f32[8,1,1,32,128]{4,3,2,1,0:T(8,128)S(1)}, f32[8,1,1,32,128]{4,3,2,1,0:T(8,128)}, u32[]{:S(2)}) copy-start(f32[8,1,1,32,128]{4,3,2,1,0:T(8,128)} %param.3) | copy-start | bytes 393220
  0.9 0.7 %copy-start.1 = (s32[1,1,32,128]{3,2,1,0:T(8,128)S(1)}, s32[1,1,32,128]{3,2,1,0:T(8,128)}, u32[]{:S(2)}) copy-start(s32[1,1,32,128]{3,2,1,0:T(8,128)} %param.4) | copy-start | bytes 49156
  2.6 15.5 %all-to-all-start = ((f32[32,8,128]{2,1,0:T(8,128)}), f32[32,8,128]{2,1,0:T(8,128)S(1)}, u32[]{:S(2)}, u32[]{:S(2)}) async-start(f32[32,8,128]{2,1,0:T(8,128)} %pack.1), calls=%async_computation | async-start | bytes 262144 | tf_op jit(solution)/shard_map/all_to_all | solution.py:149

commit v3 on v1

--- a/solution.py
+++ b/solution.py
@@ -16,26 +16,65 @@
     return factor * math.cos(math.pi * (2 * position + 1) * frequency / 8.0)
 
 
+def swap_halves(values):
+    half = values.shape[1] // 2
+    if values.shape[1] % 128 == 0:
+        return pltpu.roll(values, half, 1)
+    return jnp.concatenate([values[:, half:], values[:, :half]], axis=1)
+
+
 def pack_kernel(coef_ref, keep_ref, out_ref, *, tiles, depths):
-    slots, columns, rows = coef_ref.shape
+    _, columns, rows = coef_ref.shape
     strip = columns // tiles
     band = rows // depths
-    slot_index = lax.broadcasted_iota(jnp.int32, (slots, rows), 0)
-    for t in range(tiles):
-        masked = []
-        for b in range(strip):
-            c = t * strip + b
-            keep = jnp.broadcast_to(keep_ref[pl.ds(c, 1), :], (slots, rows))
-            masked.append(jnp.where(slot_index < keep, coef_ref[:, c, :], 0.0))
-        for d in range(depths):
-            out_ref[d * tiles + t] = jnp.concatenate(
-                [m[:, d * band : (d + 1) * band] for m in masked], axis=1
-            )
+    lane = lax.broadcasted_iota(jnp.int32, (tiles, rows), 1)
+    even = lane % 2 == 0
+
+    def take(values, index):
+        return jnp.take_along_axis(values, index, axis=1)
+
+    other = lane + 1 - 2 * (lane % 2)
+    packed = []
+    for b in range(strip):
+        mine = pl.ds(b, tiles, stride=strip)
+        keep = keep_ref[mine, :]
+        slot = [coef_ref[k, mine, :] for k in range(8)]
+        result = [slot[0]]
+        for q in (1, 2, 3, 4):
+            result.append(jnp.where(keep > q, slot[q], take(slot[8 - q], other)))
+        result[4] = jnp.where(even, result[4], (9 - keep).astype(jnp.float32))
+        packed.append(result)
+    half = strip * band // 2
+    parity = lane // half % 2
+    column = lane // (band // 2) % strip
+    source = lane % (band // 2) * 2 + parity
+    for d in range(depths):
+        for q in range(5):
+            gathered = [take(packed[b][q], source + d * band) for b in range(strip)]
+            merged = gathered[0]
+            for b in range(1, strip):
+                merged = jnp.where(column == b, gathered[b], merged)
+            out_ref[pl.ds(d * tiles, tiles), q, 0, :] = merged[:, : 2 * half]
 
 
-def render_kernel(flip_ref, coef_ref, out_ref, *, strip, band, samples):
-    zblocks, slots, lanes = coef_ref.shape
+def unpack(packed_ref, coef_ref):
+    zblocks, _, _, lanes = packed_ref.shape
+    first = lax.broadcasted_iota(jnp.int32, (zblocks, lanes), 1) < lanes // 2
+    row = [packed_ref[:, q, 0, :] for q in range(5)]
+    turned = [None] + [swap_halves(row[q]) for q in (1, 2, 3, 4)]
+    keep = jnp.where(first, turned[4], 9.0 - row[4])
+    slot = [row[0]] + [jnp.where(keep > q, row[q], 0.0) for q in (1, 2, 3)]
+    slot.append(jnp.where(keep > 4, jnp.where(first, row[4], turned[4]), 0.0))
+    slot += [jnp.where(keep > k, turned[8 - k], 0.0) for k in (5, 6, 7)]
+    for k in range(8):
+        coef_ref[k] = slot[k]
+
+
+def render_kernel(flip_ref, packed_ref, out_ref, coef_ref, *, strip, band, samples):
+    unpack(packed_ref, coef_ref)
+    slots, zblocks, lanes = coef_ref.shape
     flipped = flip_ref[0] > 0
+    sign = jnp.where(flipped, jnp.float32(-1.0), jnp.float32(1.0))
     b1 = [cosine(1, i) for i in range(EDGE)]
     row = lax.broadcasted_iota(jnp.int32, (2 * EDGE, lanes), 0)
     x = row % EDGE
@@ -51,7 +90,6 @@
     x2 = table(x, [cosine(2, i) for i in range(EDGE)])
     y1 = table(y, b1[:2])
     y2 = table(y, [cosine(2, i) for i in range(2)])
-    sign = jnp.where(flipped, jnp.float32(-1.0), jnp.float32(1.0))
     c_dc = 0.125 * LOG2E
     c_x1 = (0.25 * LOG2E) * x1
     c_x2 = (0.25 * LOG2E) * x2
@@ -67,7 +105,7 @@
     def block(step, state):
         zb = jnp.where(flipped, zblocks - 1 - step, step)
         a = [
-            jnp.broadcast_to(coef_ref[zb, pl.ds(k, 1), :], (2 * EDGE, lanes)) for k in range(slots)
+            jnp.broadcast_to(coef_ref[k, pl.ds(zb, 1), :], (2 * EDGE, lanes)) for k in range(slots)
         ]
         even = a[0] * c_dc + a[2] * c_x1 + a[4] * c_y2 + a[6] * c_x2
         odd = a[1] * c_y1 + a[5] * c_xy
@@ -101,13 +139,14 @@
     pick = lax.broadcasted_iota(jnp.int32, (2 * EDGE, width), 1)
     y_out = pick % EDGE
     place = pick // EDGE
+    place = place % 2 * (lanes // 2) + place // 2
     outs = []
     for _, before, red, green, blue in state:
         opacity = 1.0 - before
         outs.append((opacity - red, green, blue, opacity))
     for ch in range(4):
         for b in range(strip):
-            index = place + b * band
+            index = place + b * (band // 2)
             low = jnp.take_along_axis(outs[0][ch], index, axis=1)
             high = jnp.take_along_axis(outs[1][ch], index, axis=1)
             both = jnp.where(y_out < 2, low, high)
@@ -125,9 +164,10 @@
     zblocks = tiles * depths
     vmem = pl.BlockSpec(memory_space=pltpu.VMEM)
     smem = pl.BlockSpec(memory_space=pltpu.SMEM)
+    lanes = strip * band
     outgoing = pl.pallas_call(
         lambda *refs: pack_kernel(*refs, tiles=tiles, depths=depths),
-        out_shape=jax.ShapeDtypeStruct((zblocks, slots, strip * band), jnp.float32),
+        out_shape=jax.ShapeDtypeStruct((zblocks, 5, 1, lanes), jnp.float32),
         in_specs=[vmem, vmem],
         out_specs=vmem,
         name="pack",
@@ -138,6 +178,8 @@
         out_shape=jax.ShapeDtypeStruct((4, strip * EDGE, band * EDGE), jnp.float32),
         in_specs=[smem, vmem],
         out_specs=vmem,
+        scratch_shapes=[pltpu.VMEM((slots, zblocks, lanes), jnp.float32)],
+        compiler_params=pltpu.CompilerParams(vmem_limit_bytes=8 * 1024 * 1024),
         name="render",
     )(view_flip, arrived)
 

time: 20.9 us -> 18.9 us (0.904)
  Pallas kernels: 4.53 us -> 3.79 us
  local copies, waits for them, and re-layouts: 0.65 us -> 0 us
  waiting for transfers between devices: 7.58 us -> 6.96 us
    pallas_call x1, Pallas kernels: 2.8 us -> 2.02 us  [per_device(): pl.pallas_call(lambda *refs: render_kernel(*refs, strip=strip, band=band,...]
    unnamed x2 -> x0, local copies, waits for them, and re-layouts: 0.65 us -> none
    all_to_all x1, waiting for transfers between devices: 7.58 us -> 6.96 us  [per_device(): lax.all_to_all(outgoing, ('depth', 'tile'), split_axis=0, concat_axis=0,...]
where the time goes in v3:
time: 18.9 us; the launch traced here: 18.7 us
  starting transfers between devices  7.3 us (39%)
  waiting for transfers between devices  6.96 us (37%)
  Pallas kernels  3.79 us (20%)
  between operations  0.66 us (3%)
    all_to_all x1, starting transfers between devices, per_device(): lax.all_to_all(outgoing, ('depth', 'tile'), split_axis=0, concat_axis=0,...  7.3 us
    all_to_all x1, waiting for transfers between devices, per_device(): lax.all_to_all(outgoing, ('depth', 'tile'), split_axis=0, concat_axis=0,...  6.96 us
    pallas_call x1, Pallas kernels, per_device(): pl.pallas_call(lambda *refs: render_kernel(*refs, strip=strip, band=band,...  2.02 us
    pallas_call x1, Pallas kernels, per_device(): pl.pallas_call(lambda *refs: pack_kernel(*refs, tiles=tiles, depths=depth...  1.77 us
  transfers between devices with their start and end apart: 1, of which 1 were waited for; matrix products, arithmetic and copies ran while one was open for 0% of the time, Pallas kernels for 0%

profile of v3, /device:TPU:0, one launch (start us, length us, event | category | flops | bytes accessed | tf_op | source)
XLA Modules:
  0.0 18.7 jit_solution(15310853613880361574)
XLA Ops:
  0.0 1.8 %pack.1 = f32[32,5,1,128]{3,2,1,0:T(1,128)} custom-call(f32[8,32,128]{2,1,0:T(8,128)} %bitcast.2, s32[32,128]{1,0:T(8,128)} %bitcast.3), custom_call_target="tpu_custom_call" | custom-call | tf_op jit(solution)/shard_map/pack/pallas_call | solution.py:168
  1.8 7.3 %all-to-all-start = ((f32[32,5,1,128]{3,2,1,0:T(1,128)}), f32[32,5,1,128]{3,2,1,0:T(1,128)S(1)}, u32[]{:S(2)}, u32[]{:S(2)}) async-start(f32[32,5,1,128]{3,2,1,0:T(1,128)} %pack.1), calls=%async_computation | async-start | bytes 163840 | tf_op jit(solution)/shard_map/all_to_all | solution.py:175
  9.7 7.0 %all-to-all-done.refs_1_ = f32[32,5,1,128]{3,2,1,0:T(1,128)S(1)} async-done(((f32[32,5,1,128]{3,2,1,0:T(1,128)}), f32[32,5,1,128]{3,2,1,0:T(1,128)S(1)}, u32[]{:S(2)}, u32[]{:S(2)}) %all-to-all-start) | async-done | bytes 81952 | tf_op jit(solution)/shard_map/all_to_all | solution.py:175
  16.7 2.0 %render.1 = f32[4,16,128]{2,1,0:T(8,128)} custom-call(s32[1]{0:T(128)S(6)} %copy.4.refs_0_, f32[32,5,1,128]{3,2,1,0:T(1,128)S(1)} %all-to-all-done.refs_1_), custom_call_target="tpu_custom_call" | custom-call | tf_op jit(solution)/shard_map/render/pallas_call | solution.py:176
Async XLA Ops:
  1.8 14.9 %all-to-all-start = ((f32[32,5,1,128]{3,2,1,0:T(1,128)}), f32[32,5,1,128]{3,2,1,0:T(1,128)S(1)}, u32[]{:S(2)}, u32[]{:S(2)}) async-start(f32[32,5,1,128]{3,2,1,0:T(1,128)} %pack.1), calls=%async_computation | async-start | bytes 163840 | tf_op jit(solution)/shard_map/all_to_all | solution.py:175

commit v4 on v3

--- a/solution.py
+++ b/solution.py
@@ -124,9 +124,9 @@
                 after = jnp.exp2(fade * depth)
                 weight = before - after
                 before = after
-                red = red + weight / one_u
+                red = red + weight * pl.reciprocal(one_u, approx=True)
                 green = green + weight * jnp.exp2(f * (f * (-1.0 / LOG2E)))
-                blue = blue + weight / (1.0 + blue_factor * v)
+                blue = blue + weight * pl.reciprocal(1.0 + blue_factor * v, approx=True)
             halves.append((depth, before, red, green, blue))
         return tuple(halves)
 

time: 18.9 us -> 18.9 us (level)
  no operation moved by 1% of the time
where the time goes in v4:
time: 18.9 us; the launch traced here: 18.7 us
  starting transfers between devices  7.3 us (39%)
  waiting for transfers between devices  6.96 us (37%)
  Pallas kernels  3.79 us (20%)
  between operations  0.66 us (3%)
    all_to_all x1, starting transfers between devices, per_device(): lax.all_to_all(outgoing, ('depth', 'tile'), split_axis=0, concat_axis=0,...  7.3 us
    all_to_all x1, waiting for transfers between devices, per_device(): lax.all_to_all(outgoing, ('depth', 'tile'), split_axis=0, concat_axis=0,...  6.96 us
    pallas_call x1, Pallas kernels, per_device(): pl.pallas_call(lambda *refs: render_kernel(*refs, strip=strip, band=band,...  2.02 us
    pallas_call x1, Pallas kernels, per_device(): pl.pallas_call(lambda *refs: pack_kernel(*refs, tiles=tiles, depths=depth...  1.77 us
  transfers between devices with their start and end apart: 1, of which 1 were waited for; matrix products, arithmetic and copies ran while one was open for 0% of the time, Pallas kernels for 0%

profile of v4, /device:TPU:0, one launch (start us, length us, event | category | flops | bytes accessed | tf_op | source)
XLA Modules:
  0.0 18.7 jit_solution(15310853613880361574)
XLA Ops:
  0.0 1.8 %pack.1 = f32[32,5,1,128]{3,2,1,0:T(1,128)} custom-call(f32[8,32,128]{2,1,0:T(8,128)} %bitcast.2, s32[32,128]{1,0:T(8,128)} %bitcast.3), custom_call_target="tpu_custom_call" | custom-call | tf_op jit(solution)/shard_map/pack/pallas_call | solution.py:168
  1.8 7.3 %all-to-all-start = ((f32[32,5,1,128]{3,2,1,0:T(1,128)}), f32[32,5,1,128]{3,2,1,0:T(1,128)S(1)}, u32[]{:S(2)}, u32[]{:S(2)}) async-start(f32[32,5,1,128]{3,2,1,0:T(1,128)} %pack.1), calls=%async_computation | async-start | bytes 163840 | tf_op jit(solution)/shard_map/all_to_all | solution.py:175
  9.7 7.0 %all-to-all-done.refs_1_ = f32[32,5,1,128]{3,2,1,0:T(1,128)S(1)} async-done(((f32[32,5,1,128]{3,2,1,0:T(1,128)}), f32[32,5,1,128]{3,2,1,0:T(1,128)S(1)}, u32[]{:S(2)}, u32[]{:S(2)}) %all-to-all-start) | async-done | bytes 81952 | tf_op jit(solution)/shard_map/all_to_all | solution.py:175
  16.7 2.0 %render.1 = f32[4,16,128]{2,1,0:T(8,128)} custom-call(s32[1]{0:T(128)S(6)} %copy.4.refs_0_, f32[32,5,1,128]{3,2,1,0:T(1,128)S(1)} %all-to-all-done.refs_1_), custom_call_target="tpu_custom_call" | custom-call | tf_op jit(solution)/shard_map/render/pallas_call | solution.py:176
Async XLA Ops:
  1.8 14.9 %all-to-all-start = ((f32[32,5,1,128]{3,2,1,0:T(1,128)}), f32[32,5,1,128]{3,2,1,0:T(1,128)S(1)}, u32[]{:S(2)}, u32[]{:S(2)}) async-start(f32[32,5,1,128]{3,2,1,0:T(1,128)} %pack.1), calls=%async_computation | async-start | bytes 163840 | tf_op jit(solution)/shard_map/all_to_all | solution.py:175

commit v5 on v3

--- a/solution.py
+++ b/solution.py
@@ -23,7 +23,7 @@
     return jnp.concatenate([values[:, half:], values[:, :half]], axis=1)
 
 
-def pack_kernel(coef_ref, keep_ref, out_ref, *, tiles, depths):
+def pack_kernel(coef_ref, keep_ref, *out_refs, tiles, depths):
     _, columns, rows = coef_ref.shape
     strip = columns // tiles
     band = rows // depths
@@ -48,31 +48,55 @@
     parity = lane // half % 2
     column = lane // (band // 2) % strip
     source = lane % (band // 2) * 2 + parity
-    for d in range(depths):
+    me = lax.axis_index("depth")
+    for m in range(depths):
+        d = me ^ m
         for q in range(5):
             gathered = [take(packed[b][q], source + d * band) for b in range(strip)]
             merged = gathered[0]
             for b in range(1, strip):
                 merged = jnp.where(column == b, gathered[b], merged)
-            out_ref[pl.ds(d * tiles, tiles), q, 0, :] = merged[:, : 2 * half]
-
-
-def unpack(packed_ref, coef_ref):
-    zblocks, _, _, lanes = packed_ref.shape
+            out_refs[m][:, q, 0, :] = merged[:, : 2 * half]
+
+
+def chips_kernel(*refs, pairs):
+    depths = len(refs) - pairs
+    me = lax.axis_index("tile") // 2
+    for n in range(pairs):
+        for m in range(depths):
+            refs[depths + n][m] = refs[m][pl.ds((me ^ n) * 2, 2)]
+
+
+def cores_kernel(*refs):
+    pairs = len(refs) - 2
+    me = lax.axis_index("tile") % 2
+    for n in range(pairs):
+        for m in range(refs[n].shape[0]):
+            for other in range(2):
+                refs[pairs + other][n, m] = refs[n][m, me ^ other]
+
+
+def unpack(packed_refs, coef_ref):
+    pairs, depths, _, _, lanes = packed_refs[0].shape
+    zblocks = pairs * depths
     first = lax.broadcasted_iota(jnp.int32, (zblocks, lanes), 1) < lanes // 2
-    row = [packed_ref[:, q, 0, :] for q in range(5)]
-    turned = [None] + [swap_halves(row[q]) for q in (1, 2, 3, 4)]
-    keep = jnp.where(first, turned[4], 9.0 - row[4])
-    slot = [row[0]] + [jnp.where(keep > q, row[q], 0.0) for q in (1, 2, 3)]
-    slot.append(jnp.where(keep > 4, jnp.where(first, row[4], turned[4]), 0.0))
-    slot += [jnp.where(keep > k, turned[8 - k], 0.0) for k in (5, 6, 7)]
-    for k in range(8):
-        coef_ref[k] = slot[k]
-
-
-def render_kernel(flip_ref, packed_ref, out_ref, coef_ref, *, strip, band, samples):
-    unpack(packed_ref, coef_ref)
+    for other in range(2):
+        row = [packed_refs[other][:, :, q, 0, :].reshape(zblocks, lanes) for q in range(5)]
+        turned = [None] + [swap_halves(row[q]) for q in (1, 2, 3, 4)]
+        keep = jnp.where(first, turned[4], 9.0 - row[4])
+        slot = [row[0]] + [jnp.where(keep > q, row[q], 0.0) for q in (1, 2, 3)]
+        slot.append(jnp.where(keep > 4, jnp.where(first, row[4], turned[4]), 0.0))
+        slot += [jnp.where(keep > k, turned[8 - k], 0.0) for k in (5, 6, 7)]
+        for k in range(8):
+            coef_ref[k, pl.ds(other * zblocks, zblocks), :] = slot[k]
+
+
+def render_kernel(flip_ref, own_ref, other_ref, out_ref, coef_ref, *, strip, band, samples):
+    unpack((own_ref, other_ref), coef_ref)
     slots, zblocks, lanes = coef_ref.shape
+    pairs, depths = own_ref.shape[:2]
+    tile = lax.axis_index("tile")
+    depth_index = lax.axis_index("depth")
     flipped = flip_ref[0] > 0
     sign = jnp.where(flipped, jnp.float32(-1.0), jnp.float32(1.0))
     b1 = [cosine(1, i) for i in range(EDGE)]
@@ -103,7 +127,9 @@
     fade = -1.5 / samples
 
     def block(step, state):
-        zb = jnp.where(flipped, zblocks - 1 - step, step)
+        source = jnp.where(flipped, zblocks - 1 - step, step)
+        t = (source % (2 * pairs)) ^ tile
+        zb = ((t % 2) * pairs + t // 2) * depths + ((source // (2 * pairs)) ^ depth_index)
         a = [
             jnp.broadcast_to(coef_ref[k, pl.ds(zb, 1), :], (2 * EDGE, lanes)) for k in range(slots)
         ]
@@ -165,23 +191,53 @@
     vmem = pl.BlockSpec(memory_space=pltpu.VMEM)
     smem = pl.BlockSpec(memory_space=pltpu.SMEM)
     lanes = strip * band
-    outgoing = pl.pallas_call(
+    params = pltpu.CompilerParams(vmem_limit_bytes=8 * 1024 * 1024)
+    pairs = tiles // 2
+
+    def shaped(*dims):
+        return jax.ShapeDtypeStruct((*dims, 5, 1, lanes), jnp.float32)
+
+    def partners(axis, change):
+        return [(i, i ^ change) for i in range(lax.axis_size(axis))]
+
+    def swap(values, axis, change):
+        return lax.ppermute(values, axis, partners(axis, change))
+
+    parts = pl.pallas_call(
         lambda *refs: pack_kernel(*refs, tiles=tiles, depths=depths),
-        out_shape=jax.ShapeDtypeStruct((zblocks, 5, 1, lanes), jnp.float32),
+        out_shape=[shaped(tiles)] * depths,
         in_specs=[vmem, vmem],
-        out_specs=vmem,
+        out_specs=[vmem] * depths,
+        compiler_params=params,
         name="pack",
     )(coefficients.reshape(slots, columns, rows), keep_count.reshape(columns, rows))
-    arrived = lax.all_to_all(outgoing, ("depth", "tile"), split_axis=0, concat_axis=0, tiled=True)
+    parts = [parts[0]] + [swap(parts[m], "depth", m) for m in range(1, depths)]
+    parts = pl.pallas_call(
+        lambda *refs: chips_kernel(*refs, pairs=pairs),
+        out_shape=[shaped(depths, 2)] * pairs,
+        in_specs=[vmem] * depths,
+        out_specs=[vmem] * pairs,
+        compiler_params=params,
+        name="chips",
+    )(*parts)
+    parts = [parts[0]] + [swap(parts[n], "tile", 2 * n) for n in range(1, pairs)]
+    own, other = pl.pallas_call(
+        cores_kernel,
+        out_shape=[shaped(pairs, depths)] * 2,
+        in_specs=[vmem] * pairs,
+        out_specs=[vmem] * 2,
+        compiler_params=params,
+        name="cores",
+    )(*parts)
     return pl.pallas_call(
         lambda *refs: render_kernel(*refs, strip=strip, band=band, samples=EDGE * zblocks),
         out_shape=jax.ShapeDtypeStruct((4, strip * EDGE, band * EDGE), jnp.float32),
-        in_specs=[smem, vmem],
+        in_specs=[smem, vmem, vmem],
         out_specs=vmem,
         scratch_shapes=[pltpu.VMEM((slots, zblocks, lanes), jnp.float32)],
-        compiler_params=pltpu.CompilerParams(vmem_limit_bytes=8 * 1024 * 1024),
+        compiler_params=params,
         name="render",
-    )(view_flip, arrived)
+    )(view_flip, own, swap(other, "tile", 1))
 
 
 def solution(mesh):

time: 18.9 us -> 24.6 us (1.30)
  waiting for transfers between devices: 6.96 us -> 10.3 us
  starting transfers between devices: 7.3 us -> 9.3 us
  local copies, waits for them, and re-layouts: 0 us -> 1.62 us
  Pallas kernels: 3.79 us -> 2.37 us
    ppermute x0 -> x7, waiting for transfers between devices: none -> 10.3 us  [swap(): return lax.ppermute(values, axis, partners(axis, change))]
    ppermute x0 -> x7, starting transfers between devices: none -> 9.3 us  [swap(): return lax.ppermute(values, axis, partners(axis, change))]
    all_to_all x1 -> x0, starting transfers between devices: 7.3 us -> none  [per_device(): lax.all_to_all(outgoing, ('depth', 'tile'), split_axis=0, concat_axis=0,...]
    all_to_all x1 -> x0, waiting for transfers between devices: 6.96 us -> none  [per_device(): lax.all_to_all(outgoing, ('depth', 'tile'), split_axis=0, concat_axis=0,...]
    unnamed x0 -> x4, local copies, waits for them, and re-layouts: none -> 1.62 us
    pallas_call x1, Pallas kernels: 1.77 us -> 0.24 us  [per_device(): pl.pallas_call(lambda *refs: pack_kernel(*refs, tiles=tiles, depths=depth...]
  transfers between devices with their start and end apart: 1 -> 7, of which waited for: 1 -> 6; matrix products, arithmetic and copies ran while one was open for 0% -> 0% of each run, Pallas kernels for 0% -> 0%
where the time goes in v5:
time: 24.6 us; the launch traced here: 24.3 us
  waiting for transfers between devices  10.3 us (42%)
  starting transfers between devices  9.3 us (38%)
  Pallas kernels  2.37 us (10%)
  local copies, waits for them, and re-layouts  1.62 us (7%)
  between operations  0.68 us (3%)
    ppermute x7, waiting for transfers between devices, swap(): return lax.ppermute(values, axis, partners(axis, change))  10.3 us
    ppermute x7, starting transfers between devices, swap(): return lax.ppermute(values, axis, partners(axis, change))  9.3 us
    pallas_call x1, Pallas kernels, per_device(): pl.pallas_call(lambda *refs: render_kernel(*refs, strip=strip, band=band,...  2.1 us
    unnamed x4, local copies, waits for them, and re-layouts  1.62 us
  transfers between devices with their start and end apart: 7, of which 6 were waited for; matrix products, arithmetic and copies ran while one was open for 0% of the time, Pallas kernels for 0%

profile of v5, /device:TPU:0, one launch (start us, length us, event | category | flops | bytes accessed | tf_op | source)
XLA Modules:
  0.0 24.3 jit_solution(2447032670322499244)
XLA Ops:
  0.0 0.0 copy-start
  0.0 0.9 %copy-done = f32[8,1,1,32,128]{4,3,2,1,0:T(8,128)S(1)} copy-done((f32[8,1,1,32,128]{4,3,2,1,0:T(8,128)S(1)}, f32[8,1,1,32,128]{4,3,2,1,0:T(8,128)}, u32[]{:S(2)}) %copy-start) | copy-done | bytes 131096
  0.9 0.0 copy-start.1
  0.9 0.7 %copy-done.1 = s32[1,1,32,128]{3,2,1,0:T(8,128)S(1)} copy-done((s32[1,1,32,128]{3,2,1,0:T(8,128)S(1)}, s32[1,1,32,128]{3,2,1,0:T(8,128)}, u32[]{:S(2)}) %copy-start.1) | copy-done | bytes 16408
  1.6 0.2 pack.1
  1.9 3.1 %collective-permute-start = (f32[8,5,1,128]{3,2,1,0:T(1,128)S(1)}, f32[8,5,1,128]{3,2,1,0:T(1,128)S(1)}, u32[]{:S(2)}, u32[]{:S(2)}) collective-permute-start(f32[8,5,1,128]{3,2,1,0:T(1,128)S(1)} %get-tuple-element.16), channel_id=1, source_target_pairs={{0,1},{1,0},{2,3},{3,2},{4,5},{5,4},{6,7},{7,6},{8,9},{9,8},{10,11... | collective-permute-start | bytes 61448 | tf_op jit(solution)/shard_map/ppermute | solution.py:204
  5.0 2.6 %collective-permute-start.1 = (f32[8,5,1,128]{3,2,1,0:T(1,128)S(1)}, f32[8,5,1,128]{3,2,1,0:T(1,128)S(1)}, u32[]{:S(2)}, u32[]{:S(2)}) collective-permute-start(f32[8,5,1,128]{3,2,1,0:T(1,128)S(1)} %get-tuple-element.17), channel_id=1, source_target_pairs={{0,2},{1,3},{2,0},{3,1},{4,6},{5,7},{6,4},{7,5},{8,10},{9,11},{10,... | collective-permute-start | bytes 61448 | tf_op jit(solution)/shard_map/ppermute | solution.py:204
  7.6 0.0 collective-permute-start.2
  7.6 0.0 collective-permute-done.refs_1_
  7.6 2.3 %collective-permute-done.1.refs_2_ = f32[8,5,1,128]{3,2,1,0:T(1,128)S(1)} collective-permute-done((f32[8,5,1,128]{3,2,1,0:T(1,128)S(1)}, f32[8,5,1,128]{3,2,1,0:T(1,128)S(1)}, u32[]{:S(2)}, u32[]{:S(2)}) %collective-permute-start.1) | collective-permute-done | bytes 20512 | tf_op jit(solution)/shard_map/ppermute | solution.py:204
  9.9 3.3 %collective-permute-done.2.refs_3_ = f32[8,5,1,128]{3,2,1,0:T(1,128)S(1)} collective-permute-done((f32[8,5,1,128]{3,2,1,0:T(1,128)S(1)}, f32[8,5,1,128]{3,2,1,0:T(1,128)S(1)}, u32[]{:S(2)}, u32[]{:S(2)}) %collective-permute-start.2) | collective-permute-done | bytes 20512 | tf_op jit(solution)/shard_map/ppermute | solution.py:204
  13.1 1.6 %collective-permute-start.3 = (f32[4,2,5,1,128]{4,3,2,1,0:T(1,128)S(1)}, f32[4,2,5,1,128]{4,3,2,1,0:T(1,128)S(1)}, u32[]{:S(2)}, u32[]{:S(2)}) collective-permute-start(f32[4,2,5,1,128]{4,3,2,1,0:T(1,128)S(1)} %get-tuple-element.20), channel_id=1, source_target_pairs={{0,8},{4,12},{8,0},{12,4},{16,24},{20,28},{24,16},{28,20},{1,9},{5... | collective-permute-start | bytes 61448 | tf_op jit(solution)/shard_map/ppermute | solution.py:204
  14.7 1.5 %collective-permute-start.4 = (f32[4,2,5,1,128]{4,3,2,1,0:T(1,128)S(1)}, f32[4,2,5,1,128]{4,3,2,1,0:T(1,128)S(1)}, u32[]{:S(2)}, u32[]{:S(2)}) collective-permute-start(f32[4,2,5,1,128]{4,3,2,1,0:T(1,128)S(1)} %get-tuple-element.21), channel_id=1, source_target_pairs={{0,16},{4,20},{8,24},{12,28},{16,0},{20,4},{24,8},{28,12},{1,17},{... | collective-permute-start | bytes 61448 | tf_op jit(solution)/shard_map/ppermute | solution.py:204
  16.2 0.5 %collective-permute-start.5 = (f32[4,2,5,1,128]{4,3,2,1,0:T(1,128)S(1)}, f32[4,2,5,1,128]{4,3,2,1,0:T(1,128)S(1)}, u32[]{:S(2)}, u32[]{:S(2)}) collective-permute-start(f32[4,2,5,1,128]{4,3,2,1,0:T(1,128)S(1)} %get-tuple-element.22), channel_id=1, source_target_pairs={{0,24},{4,28},{8,16},{12,20},{16,8},{20,12},{24,0},{28,4},{1,25},{... | collective-permute-start | bytes 61448 | tf_op jit(solution)/shard_map/ppermute | solution.py:204
  16.7 0.3 %collective-permute-done.3.refs_1_ = f32[4,2,5,1,128]{4,3,2,1,0:T(1,128)S(1)} collective-permute-done((f32[4,2,5,1,128]{4,3,2,1,0:T(1,128)S(1)}, f32[4,2,5,1,128]{4,3,2,1,0:T(1,128)S(1)}, u32[]{:S(2)}, u32[]{:S(2)}) %collective-permute-start.3) | collective-permute-done | bytes 20512 | tf_op jit(solution)/shard_map/ppermute | solution.py:204
  17.0 1.5 %collective-permute-done.4.refs_2_ = f32[4,2,5,1,128]{4,3,2,1,0:T(1,128)S(1)} collective-permute-done((f32[4,2,5,1,128]{4,3,2,1,0:T(1,128)S(1)}, f32[4,2,5,1,128]{4,3,2,1,0:T(1,128)S(1)}, u32[]{:S(2)}, u32[]{:S(2)}) %collective-permute-start.4) | collective-permute-done | bytes 20512 | tf_op jit(solution)/shard_map/ppermute | solution.py:204
  18.5 2.4 %collective-permute-done.5.refs_3_ = f32[4,2,5,1,128]{4,3,2,1,0:T(1,128)S(1)} collective-permute-done((f32[4,2,5,1,128]{4,3,2,1,0:T(1,128)S(1)}, f32[4,2,5,1,128]{4,3,2,1,0:T(1,128)S(1)}, u32[]{:S(2)}, u32[]{:S(2)}) %collective-permute-start.5) | collective-permute-done | bytes 20512 | tf_op jit(solution)/shard_map/ppermute | solution.py:204
  20.9 0.1 collective-permute-start.6
  21.7 0.6 %collective-permute-done.6.refs_2_ = f32[4,4,5,1,128]{4,3,2,1,0:T(1,128)S(1)} collective-permute-done((f32[4,4,5,1,128]{4,3,2,1,0:T(1,128)S(1)}, f32[4,4,5,1,128]{4,3,2,1,0:T(1,128)S(1)}, u32[]{:S(2)}, u32[]{:S(2)}) %collective-permute-start.6) | collective-permute-done | bytes 40992 | tf_op jit(solution)/shard_map/ppermute | solution.py:204
  22.2 2.1 %render.1 = f32[4,16,128]{2,1,0:T(8,128)} custom-call(s32[1]{0:T(128)S(6)} %copy.4.refs_0_, f32[4,4,5,1,128]{4,3,2,1,0:T(1,128)S(1)} %get-tuple-element.23.refs_1_, f32[4,4,5,1,128]{4,3,2,1,0:T(1,128)S(1)} %collective-permute-done.6.refs_2_), custom_call_target="tpu_custom_call" | custom-call | tf_op jit(solution)/shard_map/render/pallas_call | solution.py:232
  (2 shorter events, 0.0 us)
Async XLA Ops:
  0.0 0.9 %copy-start = (f32[8,1,1,32,128]{4,3,2,1,0:T(8,128)S(1)}, f32[8,1,1,32,128]{4,3,2,1,0:T(8,128)}, u32[]{:S(2)}) copy-start(f32[8,1,1,32,128]{4,3,2,1,0:T(8,128)} %param.3) | copy-start | bytes 393220
  0.9 0.7 %copy-start.1 = (s32[1,1,32,128]{3,2,1,0:T(8,128)S(1)}, s32[1,1,32,128]{3,2,1,0:T(8,128)}, u32[]{:S(2)}) copy-start(s32[1,1,32,128]{3,2,1,0:T(8,128)} %param.4) | copy-start | bytes 49156
  1.9 5.7 %collective-permute-start = (f32[8,5,1,128]{3,2,1,0:T(1,128)S(1)}, f32[8,5,1,128]{3,2,1,0:T(1,128)S(1)}, u32[]{:S(2)}, u32[]{:S(2)}) collective-permute-start(f32[8,5,1,128]{3,2,1,0:T(1,128)S(1)} %get-tuple-element.16), channel_id=1, source_target_pairs={{0,1},{1,0},{2,3},{3,2},{4,5},{5,4},{6,7},{7,6},{8,9},{9,8},{10,11... | collective-permute-start | bytes 61448 | tf_op jit(solution)/shard_map/ppermute | solution.py:204
  5.0 4.9 %collective-permute-start.1 = (f32[8,5,1,128]{3,2,1,0:T(1,128)S(1)}, f32[8,5,1,128]{3,2,1,0:T(1,128)S(1)}, u32[]{:S(2)}, u32[]{:S(2)}) collective-permute-start(f32[8,5,1,128]{3,2,1,0:T(1,128)S(1)} %get-tuple-element.17), channel_id=1, source_target_pairs={{0,2},{1,3},{2,0},{3,1},{4,6},{5,7},{6,4},{7,5},{8,10},{9,11},{10,... | collective-permute-start | bytes 61448 | tf_op jit(solution)/shard_map/ppermute | solution.py:204
  7.6 5.6 %collective-permute-start.2 = (f32[8,5,1,128]{3,2,1,0:T(1,128)S(1)}, f32[8,5,1,128]{3,2,1,0:T(1,128)S(1)}, u32[]{:S(2)}, u32[]{:S(2)}) collective-permute-start(f32[8,5,1,128]{3,2,1,0:T(1,128)S(1)} %get-tuple-element.18), channel_id=1, source_target_pairs={{0,3},{1,2},{2,1},{3,0},{4,7},{5,6},{6,5},{7,4},{8,11},{9,10},{10,... | collective-permute-start | bytes 61448 | tf_op jit(solution)/shard_map/ppermute | solution.py:204
  13.1 3.8 %collective-permute-start.3 = (f32[4,2,5,1,128]{4,3,2,1,0:T(1,128)S(1)}, f32[4,2,5,1,128]{4,3,2,1,0:T(1,128)S(1)}, u32[]{:S(2)}, u32[]{:S(2)}) collective-permute-start(f32[4,2,5,1,128]{4,3,2,1,0:T(1,128)S(1)} %get-tuple-element.20), channel_id=1, source_target_pairs={{0,8},{4,12},{8,0},{12,4},{16,24},{20,28},{24,16},{28,20},{1,9},{5... | collective-permute-start | bytes 61448 | tf_op jit(solution)/shard_map/ppermute | solution.py:204
  14.7 3.8 %collective-permute-start.4 = (f32[4,2,5,1,128]{4,3,2,1,0:T(1,128)S(1)}, f32[4,2,5,1,128]{4,3,2,1,0:T(1,128)S(1)}, u32[]{:S(2)}, u32[]{:S(2)}) collective-permute-start(f32[4,2,5,1,128]{4,3,2,1,0:T(1,128)S(1)} %get-tuple-element.21), channel_id=1, source_target_pairs={{0,16},{4,20},{8,24},{12,28},{16,0},{20,4},{24,8},{28,12},{1,17},{... | collective-permute-start | bytes 61448 | tf_op jit(solution)/shard_map/ppermute | solution.py:204
  16.2 4.7 %collective-permute-start.5 = (f32[4,2,5,1,128]{4,3,2,1,0:T(1,128)S(1)}, f32[4,2,5,1,128]{4,3,2,1,0:T(1,128)S(1)}, u32[]{:S(2)}, u32[]{:S(2)}) collective-permute-start(f32[4,2,5,1,128]{4,3,2,1,0:T(1,128)S(1)} %get-tuple-element.22), channel_id=1, source_target_pairs={{0,24},{4,28},{8,16},{12,20},{16,8},{20,12},{24,0},{28,4},{1,25},{... | collective-permute-start | bytes 61448 | tf_op jit(solution)/shard_map/ppermute | solution.py:204
  20.9 1.3 %collective-permute-start.6 = (f32[4,4,5,1,128]{4,3,2,1,0:T(1,128)S(1)}, f32[4,4,5,1,128]{4,3,2,1,0:T(1,128)S(1)}, u32[]{:S(2)}, u32[]{:S(2)}) collective-permute-start(f32[4,4,5,1,128]{4,3,2,1,0:T(1,128)S(1)} %get-tuple-element.24), channel_id=1, source_target_pairs={{0,4},{4,0},{8,12},{12,8},{16,20},{20,16},{24,28},{28,24},{1,5},{5... | collective-permute-start | bytes 122888 | tf_op jit(solution)/shard_map/ppermute | solution.py:204

commit v6 on v3

--- a/solution.py
+++ b/solution.py
@@ -23,10 +23,16 @@
     return jnp.concatenate([values[:, half:], values[:, :half]], axis=1)
 
 
-def pack_kernel(coef_ref, keep_ref, out_ref, *, tiles, depths):
+def pack_kernel(coef_hbm, keep_hbm, out_ref, coef_ref, keep_ref, arrival, *, tiles, depths):
     _, columns, rows = coef_ref.shape
     strip = columns // tiles
     band = rows // depths
+    moves = ((coef_hbm, coef_ref), (keep_hbm, keep_ref))
+    fetches = [pltpu.make_async_copy(a, b, arrival.at[i]) for i, (a, b) in enumerate(moves)]
+    for fetch in fetches:
+        fetch.start()
+    for fetch in fetches:
+        fetch.wait()
     lane = lax.broadcasted_iota(jnp.int32, (tiles, rows), 1)
     even = lane % 2 == 0
 
@@ -163,23 +169,30 @@
     band = rows // depths
     zblocks = tiles * depths
     vmem = pl.BlockSpec(memory_space=pltpu.VMEM)
-    smem = pl.BlockSpec(memory_space=pltpu.SMEM)
+    params = pltpu.CompilerParams(vmem_limit_bytes=8 * 1024 * 1024)
     lanes = strip * band
+    inputs = (coefficients.reshape(slots, columns, rows), keep_count.reshape(columns, rows))
     outgoing = pl.pallas_call(
         lambda *refs: pack_kernel(*refs, tiles=tiles, depths=depths),
-        out_shape=jax.ShapeDtypeStruct((zblocks, 5, 1, lanes), jnp.float32),
-        in_specs=[vmem, vmem],
+        out_shape=pltpu.VMEM((zblocks, 5, 1, lanes), jnp.float32),
+        in_specs=[pl.BlockSpec(memory_space=pltpu.HBM)] * 2,
         out_specs=vmem,
+        scratch_shapes=[
+            pltpu.VMEM((slots, columns, rows), jnp.float32),
+            pltpu.VMEM((columns, rows), jnp.int32),
+            pltpu.SemaphoreType.DMA((2,)),
+        ],
+        compiler_params=params,
         name="pack",
-    )(coefficients.reshape(slots, columns, rows), keep_count.reshape(columns, rows))
+    )(*(pltpu.with_memory_space_constraint(x, pltpu.HBM) for x in inputs))
     arrived = lax.all_to_all(outgoing, ("depth", "tile"), split_axis=0, concat_axis=0, tiled=True)
     return pl.pallas_call(
         lambda *refs: render_kernel(*refs, strip=strip, band=band, samples=EDGE * zblocks),
         out_shape=jax.ShapeDtypeStruct((4, strip * EDGE, band * EDGE), jnp.float32),
-        in_specs=[smem, vmem],
+        in_specs=[pl.BlockSpec(memory_space=pltpu.SMEM), vmem],
         out_specs=vmem,
         scratch_shapes=[pltpu.VMEM((slots, zblocks, lanes), jnp.float32)],
-        compiler_params=pltpu.CompilerParams(vmem_limit_bytes=8 * 1024 * 1024),
+        compiler_params=params,
         name="render",
     )(view_flip, arrived)
 

time: 18.9 us -> 18.9 us (level)
  no operation moved by 1% of the time
where the time goes in v6:
time: 18.9 us; the launch traced here: 18.7 us
  starting transfers between devices  7.3 us (39%)
  waiting for transfers between devices  6.96 us (37%)
  Pallas kernels  3.8 us (20%)
  between operations  0.66 us (3%)
    all_to_all x1, starting transfers between devices, per_device(): lax.all_to_all(outgoing, ('depth', 'tile'), split_axis=0, concat_axis=0,...  7.3 us
    all_to_all x1, waiting for transfers between devices, per_device(): lax.all_to_all(outgoing, ('depth', 'tile'), split_axis=0, concat_axis=0,...  6.96 us
    pallas_call x1, Pallas kernels, per_device(): pl.pallas_call(lambda *refs: render_kernel(*refs, strip=strip, band=band,...  2.02 us
    pallas_call x1, Pallas kernels, per_device(): pl.pallas_call(lambda *refs: pack_kernel(*refs, tiles=tiles, depths=depth...  1.78 us
  transfers between devices with their start and end apart: 1, of which 1 were waited for; matrix products, arithmetic and copies ran while one was open for 0% of the time, Pallas kernels for 0%

profile of v6, /device:TPU:0, one launch (start us, length us, event | category | flops | bytes accessed | tf_op | source)
XLA Modules:
  0.0 18.7 jit_solution(9923241270145942976)
XLA Ops:
  0.0 1.8 %pack.1 = f32[32,5,1,128]{3,2,1,0:T(1,128)} custom-call(f32[8,32,128]{2,1,0:T(8,128)} %bitcast.2, s32[32,128]{1,0:T(8,128)} %bitcast.3), custom_call_target="tpu_custom_call" | custom-call | tf_op jit(solution)/shard_map/pack/pallas_call | solution.py:175
  1.8 7.3 %all-to-all-start = ((f32[32,5,1,128]{3,2,1,0:T(1,128)}), f32[32,5,1,128]{3,2,1,0:T(1,128)S(1)}, u32[]{:S(2)}, u32[]{:S(2)}) async-start(f32[32,5,1,128]{3,2,1,0:T(1,128)} %pack.1), calls=%async_computation | async-start | bytes 163840 | tf_op jit(solution)/shard_map/all_to_all | solution.py:188
  9.8 7.0 %all-to-all-done.refs_1_ = f32[32,5,1,128]{3,2,1,0:T(1,128)S(1)} async-done(((f32[32,5,1,128]{3,2,1,0:T(1,128)}), f32[32,5,1,128]{3,2,1,0:T(1,128)S(1)}, u32[]{:S(2)}, u32[]{:S(2)}) %all-to-all-start) | async-done | bytes 81952 | tf_op jit(solution)/shard_map/all_to_all | solution.py:188
  16.7 2.0 %render.1 = f32[4,16,128]{2,1,0:T(8,128)} custom-call(s32[1]{0:T(128)S(6)} %copy.4.refs_0_, f32[32,5,1,128]{3,2,1,0:T(1,128)S(1)} %all-to-all-done.refs_1_), custom_call_target="tpu_custom_call" | custom-call | tf_op jit(solution)/shard_map/render/pallas_call | solution.py:189
Async XLA Ops:
  1.8 14.9 %all-to-all-start = ((f32[32,5,1,128]{3,2,1,0:T(1,128)}), f32[32,5,1,128]{3,2,1,0:T(1,128)S(1)}, u32[]{:S(2)}, u32[]{:S(2)}) async-start(f32[32,5,1,128]{3,2,1,0:T(1,128)} %pack.1), calls=%async_computation | async-start | bytes 163840 | tf_op jit(solution)/shard_map/all_to_all | solution.py:188

commit v7 on v6

--- a/solution.py
+++ b/solution.py
@@ -23,7 +23,7 @@
     return jnp.concatenate([values[:, half:], values[:, :half]], axis=1)
 
 
-def pack_kernel(coef_hbm, keep_hbm, out_ref, coef_ref, keep_ref, arrival, *, tiles, depths):
+def pack_kernel(coef_hbm, keep_hbm, out_ref, coef_ref, keep_ref, rows_ref, arrival, *, tiles, depths):
     _, columns, rows = coef_ref.shape
     strip = columns // tiles
     band = rows // depths
@@ -54,16 +54,28 @@
     parity = lane // half % 2
     column = lane // (band // 2) % strip
     source = lane % (band // 2) * 2 + parity
+    chips = tiles // 2
+    core = lax.axis_index("tile") % 2
     for d in range(depths):
         for q in range(5):
             gathered = [take(packed[b][q], source + d * band) for b in range(strip)]
             merged = gathered[0]
             for b in range(1, strip):
                 merged = jnp.where(column == b, gathered[b], merged)
-            out_ref[pl.ds(d * tiles, tiles), q, 0, :] = merged[:, : 2 * half]
-
-
-def unpack(packed_ref, coef_ref):
+            rows_ref[d, q] = merged[:, : 2 * half]
+    for d in range(depths):
+        for q in range(5):
+            for other in range(2):
+                chosen = rows_ref[d, q, pl.ds(core ^ other, chips, stride=2), :]
+                out_ref[pl.ds(d * chips, chips), other, q, 0, :] = chosen
+
+
+def cores_kernel(both_ref, own_ref, other_ref):
+    own_ref[...] = both_ref[:, 0]
+    other_ref[...] = both_ref[:, 1]
+
+
+def unpack(packed_ref, coef_ref, start):
     zblocks, _, _, lanes = packed_ref.shape
     first = lax.broadcasted_iota(jnp.int32, (zblocks, lanes), 1) < lanes // 2
     row = [packed_ref[:, q, 0, :] for q in range(5)]
@@ -73,11 +85,13 @@
     slot.append(jnp.where(keep > 4, jnp.where(first, row[4], turned[4]), 0.0))
     slot += [jnp.where(keep > k, turned[8 - k], 0.0) for k in (5, 6, 7)]
     for k in range(8):
-        coef_ref[k] = slot[k]
-
-
-def render_kernel(flip_ref, packed_ref, out_ref, coef_ref, *, strip, band, samples):
-    unpack(packed_ref, coef_ref)
+        coef_ref[k, pl.ds(start, zblocks), :] = slot[k]
+
+
+def render_kernel(flip_ref, own_ref, other_ref, out_ref, coef_ref, *, strip, band, samples):
+    unpack(own_ref, coef_ref, 0)
+    unpack(other_ref, coef_ref, other_ref.shape[0])
+    core = lax.axis_index("tile") % 2
     slots, zblocks, lanes = coef_ref.shape
     flipped = flip_ref[0] > 0
     sign = jnp.where(flipped, jnp.float32(-1.0), jnp.float32(1.0))
@@ -109,7 +123,8 @@
     fade = -1.5 / samples
 
     def block(step, state):
-        zb = jnp.where(flipped, zblocks - 1 - step, step)
+        source = jnp.where(flipped, zblocks - 1 - step, step)
+        zb = (source % 2 ^ core) * (zblocks // 2) + source // 2
         a = [
             jnp.broadcast_to(coef_ref[k, pl.ds(zb, 1), :], (2 * EDGE, lanes)) for k in range(slots)
         ]
@@ -171,30 +186,44 @@
     vmem = pl.BlockSpec(memory_space=pltpu.VMEM)
     params = pltpu.CompilerParams(vmem_limit_bytes=8 * 1024 * 1024)
     lanes = strip * band
+    chips = zblocks // 2
+    same_core = [[2 * chip + core for chip in range(chips)] for core in range(2)]
     inputs = (coefficients.reshape(slots, columns, rows), keep_count.reshape(columns, rows))
     outgoing = pl.pallas_call(
         lambda *refs: pack_kernel(*refs, tiles=tiles, depths=depths),
-        out_shape=pltpu.VMEM((zblocks, 5, 1, lanes), jnp.float32),
+        out_shape=jax.ShapeDtypeStruct((chips, 2, 5, 1, lanes), jnp.float32),
         in_specs=[pl.BlockSpec(memory_space=pltpu.HBM)] * 2,
         out_specs=vmem,
         scratch_shapes=[
             pltpu.VMEM((slots, columns, rows), jnp.float32),
             pltpu.VMEM((columns, rows), jnp.int32),
+            pltpu.VMEM((depths, 5, tiles, lanes), jnp.float32),
             pltpu.SemaphoreType.DMA((2,)),
         ],
         compiler_params=params,
         name="pack",
     )(*(pltpu.with_memory_space_constraint(x, pltpu.HBM) for x in inputs))
-    arrived = lax.all_to_all(outgoing, ("depth", "tile"), split_axis=0, concat_axis=0, tiled=True)
+    arrived = lax.all_to_all(
+        outgoing, ("depth", "tile"), split_axis=0, concat_axis=0, tiled=True, axis_index_groups=same_core
+    )
+    own, other = pl.pallas_call(
+        cores_kernel,
+        out_shape=[jax.ShapeDtypeStruct((chips, 5, 1, lanes), jnp.float32)] * 2,
+        in_specs=[vmem],
+        out_specs=[vmem, vmem],
+        compiler_params=params,
+        name="cores",
+    )(arrived)
+    other = lax.ppermute(other, "tile", [(t, t ^ 1) for t in range(tiles)])
     return pl.pallas_call(
         lambda *refs: render_kernel(*refs, strip=strip, band=band, samples=EDGE * zblocks),
         out_shape=jax.ShapeDtypeStruct((4, strip * EDGE, band * EDGE), jnp.float32),
-        in_specs=[pl.BlockSpec(memory_space=pltpu.SMEM), vmem],
+        in_specs=[pl.BlockSpec(memory_space=pltpu.SMEM), vmem, vmem],
         out_specs=vmem,
         scratch_shapes=[pltpu.VMEM((slots, zblocks, lanes), jnp.float32)],
         compiler_params=params,
         name="render",
-    )(view_flip, arrived)
+    )(view_flip, own, other)
 
 
 def solution(mesh):

time: 18.9 us -> 20.5 us (1.085)
  blocking collectives: 0 us -> 15.7 us
  starting transfers between devices: 7.3 us -> 0.07 us
  waiting for transfers between devices: 6.96 us -> 0.56 us
  Pallas kernels: 3.8 us -> 3.28 us
    all_to_all x0 -> x1, blocking collectives: none -> 15.7 us  [per_device(): lax.all_to_all(outgoing, ('depth', 'tile'), split_axis=0, concat_axis=0,...]
    all_to_all x1 -> x0, starting transfers between devices: 7.3 us -> none  [per_device(): lax.all_to_all(outgoing, ('depth', 'tile'), split_axis=0, concat_axis=0,...]
    all_to_all x1 -> x0, waiting for transfers between devices: 6.96 us -> none  [per_device(): lax.all_to_all(outgoing, ('depth', 'tile'), split_axis=0, concat_axis=0,...]
    pallas_call x1, Pallas kernels: 1.78 us -> 1.2 us  [per_device(): pl.pallas_call(lambda *refs: pack_kernel(*refs, tiles=tiles, depths=depth...]
    ppermute x0 -> x1, waiting for transfers between devices: none -> 0.56 us  [per_device(): other = lax.ppermute(other, 'tile', [(t, t ^ 1) for t in range(tiles)])]
where the time goes in v7:
time: 20.5 us; the launch traced here: 20.3 us
  blocking collectives  15.7 us (77%)
  Pallas kernels  3.28 us (16%)
  between operations  0.67 us (3%)
  waiting for transfers between devices  0.56 us (3%)
    all_to_all x1, blocking collectives, per_device(): lax.all_to_all(outgoing, ('depth', 'tile'), split_axis=0, concat_axis=0,...  15.7 us
    pallas_call x1, Pallas kernels, per_device(): pl.pallas_call(lambda *refs: render_kernel(*refs, strip=strip, band=band,...  2.06 us
    pallas_call x1, Pallas kernels, per_device(): pl.pallas_call(lambda *refs: pack_kernel(*refs, tiles=tiles, depths=depth...  1.2 us
    ppermute x1, waiting for transfers between devices, per_device(): other = lax.ppermute(other, 'tile', [(t, t ^ 1) for t in range(tiles)])  0.56 us
  transfers between devices with their start and end apart: 1, of which 1 were waited for; matrix products, arithmetic and copies ran while one was open for 0% of the time, Pallas kernels for 0%

profile of v7, /device:TPU:0, one launch (start us, length us, event | category | flops | bytes accessed | tf_op | source)
XLA Modules:
  0.0 20.3 jit_solution(9675614713248440578)
XLA Ops:
  0.0 1.2 %pack.1 = f32[16,2,5,1,128]{4,3,2,1,0:T(1,128)S(1)} custom-call(f32[8,32,128]{2,1,0:T(8,128)} %bitcast.2, s32[32,128]{1,0:T(8,128)} %bitcast.3), custom_call_target="tpu_custom_call" | custom-call | tf_op jit(solution)/shard_map/pack/pallas_call | solution.py:192
  1.2 15.7 %all_to_all.5.both_ref = f32[16,2,5,1,128]{4,3,2,1,0:T(1,128)S(1)} all-to-all(f32[16,2,5,1,128]{4,3,2,1,0:T(1,128)S(1)} %pack.1), channel_id=1, replica_groups={{0,8,16,24,1,9,17,25,2,10,18,26,3,11,19,27},{4,12,20,28,5,13,21,29,6,14..., dimensions={0} | all-to-all | bytes 163840 | tf_op jit(solution)/shard_map/all_to_all | solution.py:206
  16.9 0.1 collective-permute-start
  17.7 0.6 %collective-permute-done.refs_2_ = f32[16,5,1,128]{3,2,1,0:T(1,128)S(1)} collective-permute-done((f32[16,5,1,128]{3,2,1,0:T(1,128)S(1)}, f32[16,5,1,128]{3,2,1,0:T(1,128)S(1)}, u32[]{:S(2)}, u32[]{:S(2)}) %collective-permute-start) | collective-permute-done | bytes 40992 | tf_op jit(solution)/shard_map/ppermute | solution.py:217
  18.2 2.1 %render.1 = f32[4,16,128]{2,1,0:T(8,128)} custom-call(s32[1]{0:T(128)S(6)} %copy.4.refs_0_, f32[16,5,1,128]{3,2,1,0:T(1,128)S(1)} %get-tuple-element.7.refs_1_, f32[16,5,1,128]{3,2,1,0:T(1,128)S(1)} %collective-permute-done.refs_2_), custom_call_target="tpu_custom_call" | custom-call | tf_op jit(solution)/shard_map/render/pallas_call | solution.py:218
  (1 shorter events, 0.0 us)
Async XLA Ops:
  16.9 1.3 %collective-permute-start = (f32[16,5,1,128]{3,2,1,0:T(1,128)S(1)}, f32[16,5,1,128]{3,2,1,0:T(1,128)S(1)}, u32[]{:S(2)}, u32[]{:S(2)}) collective-permute-start(f32[16,5,1,128]{3,2,1,0:T(1,128)S(1)} %get-tuple-element.8), channel_id=1, source_target_pairs={{0,4},{4,0},{8,12},{12,8},{16,20},{20,16},{24,28},{28,24},{1,5},{5... | collective-permute-start | bytes 122888 | tf_op jit(solution)/shard_map/ppermute | solution.py:217
